TPU v7x, 256 devices: a whole 4x4x8 slice. The times are simulated.
256 devices in a mesh: dp: 32 (over z, y_hi, core), tensor: 8 (over y_lo, x).
Axes of the slice: x: 4, y: 4 (y_hi: 2, y_lo: 2; y = y_hi * 2 + y_lo), z: 8, core: 2. Of those that a mesh axis runs over, the one named last changes fastest.
Arguments:
- glu_input: bfloat16 [4096, 2, 3, 1024], P('dp', None, None, 'tensor'), may hold values from -6 to 6
- conv_kernel: bfloat16 [32, 3, 1024], P(None, None, 'tensor'), may hold values from -1 to 1
- norm_gain: float32 [3, 1024], P(None, 'tensor'), may hold values from 0.5 to 2
- norm_shift: float32 [3, 1024], P(None, 'tensor'), may hold values from -3 to 3
- out_weight: bfloat16 [3, 1024, 3, 1024], P(None, 'tensor'), may hold values from -0.109375 to 0.109375
- out_cotangent: bfloat16 [4096, 3, 1024], P('dp'), may hold values from -6 to 6
- root_stack: bfloat16 [16, 2, 1024, 1024], P('tensor', None, 'dp'), as said below
- home: int32 [9], replicated, may hold values from 0 to 15, as said below
Outputs:
- glu_grad: bfloat16 [4096, 2, 3, 1024], P('dp', None, None, 'tensor')
- kernel_grad: float32 [32, 3, 1024], P(None, None, 'tensor')
- update: bfloat16 [3, 1024, 3, 1024], P(None, 'tensor')
Inputs may be any that keep to these rules, and one draw needn't show every extreme that they name: Distinct entries; tensor index home // 2 owns block b. An owner holds at most 2 blocks, and in every draw one owner holds exactly 2. `root_stack`: each of the two matrices in a slot is symmetric.
All inputs are finite; a program needn't handle non-finite values.
Results may differ from a plain program's by a relative error of at most 0.0057.
Values may be sent and summed in bfloat16 or wider, within the bound.
A program may use at most 128 MiB of HBM per device.

v0:
```python
import jax
import jax.numpy as jnp
from jax import lax
from jax.sharding import PartitionSpec as P

LEN = 2048


def padded(cells, sides, width):
    for axis, dim in sides:
        count = lax.axis_size(axis)
        ends = count - 1
        head = lax.slice_in_dim(cells, 0, width, axis=dim)
        tail = lax.slice_in_dim(cells, cells.shape[dim] - width, cells.shape[dim], axis=dim)
        cells = jnp.concatenate(
            [
                lax.ppermute(tail, axis, [(i, (i + 1) % count) for i in range(ends)]),
                cells,
                lax.ppermute(head, axis, [((i + 1) % count, i) for i in range(ends)]),
            ],
            axis=dim,
        )
    return cells


def broadcast(block, axis, holder):
    block = jnp.where(lax.axis_index(axis) == holder, block, jnp.zeros_like(block))
    return lax.psum(block, axis)


def per_device(
    glu_input, conv_kernel, norm_gain, norm_shift, out_weight, out_cotangent, root_stack, home
):
    local_tokens = glu_input.shape[0]
    kernel_len = conv_kernel.shape[0]
    half_kernel = kernel_len // 2
    n_blocks = out_weight.shape[0]
    block_len = out_cotangent.shape[2]
    tensor_rows = glu_input.shape[3]
    data_size = lax.axis_size("dp")
    col_count = block_len // data_size
    utterances = local_tokens * data_size // LEN
    lin_half = glu_input[:, 0].astype(jnp.float32)
    gate_half = glu_input[:, 1].astype(jnp.float32)
    gate_sig = jax.nn.sigmoid(gate_half)
    glu_out = (lin_half * gate_sig).astype(jnp.bfloat16)
    first_token = lax.axis_index("dp") * local_tokens
    own_utt = (first_token + LEN // 2 + jnp.arange(local_tokens, dtype=jnp.int32)) // LEN
    ext_utt = (
        first_token
        - half_kernel
        + LEN // 2
        + jnp.arange(local_tokens + kernel_len, dtype=jnp.int32)
    ) // LEN
    glu_ext = padded(glu_out, (("dp", 0),), half_kernel).astype(jnp.float32)
    kernel_f = conv_kernel.astype(jnp.float32)

    def tap_input(tap_index):
        same_utt = (ext_utt[tap_index : tap_index + local_tokens] == own_utt).astype(jnp.float32)
        return glu_ext[tap_index : tap_index + local_tokens] * same_utt[:, None, None]

    conv_out = jnp.zeros(glu_out.shape, jnp.float32)
    for tap_index in range(kernel_len):
        conv_out = conv_out + kernel_f[tap_index] * tap_input(tap_index)
    normed = conv_out * norm_gain + norm_shift
    norm_sig = jax.nn.sigmoid(normed)
    activated = (normed * norm_sig).astype(jnp.bfloat16)
    act_grad = jnp.einsum(
        "tjc,irjc->tir", out_cotangent, out_weight, preferred_element_type=jnp.float32
    )
    conv_grad = (act_grad * norm_sig * (1.0 + normed * (1.0 - norm_sig)) * norm_gain).astype(
        jnp.bfloat16
    )
    grad_ext = padded(conv_grad, (("dp", 0),), half_kernel).astype(jnp.float32)
    grad_f = conv_grad.astype(jnp.float32)
    kernel_terms = []
    input_grad = jnp.zeros(glu_out.shape, jnp.float32)
    for tap_index in range(kernel_len):
        kernel_terms.append(jnp.sum(tap_input(tap_index) * grad_f, axis=0))
        back_index = kernel_len - tap_index
        same_back = (ext_utt[back_index : back_index + local_tokens] == own_utt).astype(jnp.float32)
        input_grad = (
            input_grad
            + kernel_f[tap_index]
            * grad_ext[back_index : back_index + local_tokens]
            * same_back[:, None, None]
        )
    kernel_grad = lax.psum(jnp.stack(kernel_terms), "dp") / utterances
    glu_grad = jnp.stack(
        [input_grad * gate_sig, input_grad * lin_half * gate_sig * (1.0 - gate_sig)], axis=1
    ).astype(jnp.bfloat16)
    grad_share = (
        lax.psum_scatter(
            jnp.einsum(
                "tjc,tir->cjir", out_cotangent, activated, preferred_element_type=jnp.float32
            ),
            "dp",
            scatter_dimension=0,
            tiled=True,
        )
        / utterances
    )
    tensor_index = lax.axis_index("tensor")
    slot_count = root_stack.shape[0]
    n_pairs = home.shape[0]
    owners = home // slot_count
    slots_of = home % slot_count

    def fetch_block(block_no, fetched):
        mine = lax.dynamic_index_in_dim(root_stack, slots_of[block_no], 0, keepdims=False)
        arrived = broadcast(mine, "tensor", owners[block_no])
        return lax.dynamic_update_index_in_dim(fetched, arrived, block_no, 0)

    empty = jnp.zeros((n_pairs,) + root_stack.shape[1:], jnp.bfloat16)
    chosen = lax.fori_loop(0, n_pairs, fetch_block, empty)
    left_cols = lax.dynamic_slice_in_dim(chosen[:, 0], tensor_index * tensor_rows, tensor_rows, 2)
    left_piece = left_cols.reshape(n_blocks, n_blocks, col_count, tensor_rows).transpose(2, 0, 1, 3)
    left_full = lax.all_gather(left_piece, "dp", axis=0, tiled=True)
    rows_now = left_full.astype(jnp.float32)
    left_share = lax.psum_scatter(
        jnp.einsum("kijr,cjir->kijc", rows_now, grad_share, precision=lax.Precision.HIGHEST),
        "tensor",
        scatter_dimension=0,
        tiled=True,
    )
    right_rows = chosen[:, 1].reshape(n_blocks, n_blocks, col_count, block_len).astype(jnp.float32)
    update_term = jnp.einsum(
        "rijc,ijce->irje", left_share, right_rows, precision=lax.Precision.HIGHEST
    )
    update = lax.psum(update_term, "dp").astype(jnp.bfloat16)
    return (glu_grad, kernel_grad, update)


def solution(mesh):
    placed = (
        P("dp", None, None, "tensor"),
        P(None, None, "tensor"),
        P(None, "tensor"),
        P(None, "tensor"),
        P(None, "tensor", None, None),
        P("dp", None, None),
        P("tensor", None, "dp", None),
        P(),
    )
    return jax.shard_map(
        per_device,
        mesh=mesh,
        in_specs=placed,
        out_specs=(
            P("dp", None, None, "tensor"),
            P(None, None, "tensor"),
            P(None, "tensor", None, None),
        ),
        check_vma=False,
    )
```

profile of v0, /device:TPU:9, one launch (start us, length us, event | category | flops | bytes accessed | tf_op | source)
XLA Modules:
  0.0 1381.2 jit_solution(11933506581270610640)
XLA Ops:
  10.3 4.5 collective-permute-start
  21.5 2.5 multiply_add_fusion
  25.0 3.0 convolution_bitcast_fusion.1
  28.1 7.2 copy.31
  35.3 756.1 %while.13 = (s32[]{:T(128)}, bf16[9,2,32,1024]{3,2,1,0:T(8,128)(2,1)}, s32[9]{0:T(128)S(1)}, s32[9]{0:T(128)S(1)}, bf16[2,2,32,1024]{3,2,1,0:T(8,128)(2,1)S(1)},...) while((s32[]{:T(128)}, bf16[9,2,32,1024]{3,2,1,0:T(8,128)(2,1)}, s32[9]{0:T(128)S(1)}, s32[9]{0:T(128)S(1)}, ...), condition=%wide.region_35.36_spmd, body=%wide.region_33.35_spmd.sunk | while | flops 131080 | bytes 1310957 | solution.py:115
  39.7 76.8 %all-reduce.8.cloned.1.call-done = bf16[1,2,32,1024]{3,2,1,0:T(8,128)(2,1)} async-done(((bf16[1,2,32,1024]{3,2,1,0:T(8,128)(2,1)}), bf16[1,2,32,1024]{3,2,1,0:T(8,128)(2,1)}) %all-reduce.8.cloned.1.call-update) | async-done | bytes 131088 | tf_op jit(solution)/shard_map/while/body/eval_jaxpr/psum | solution.py:28
  122.5 78.1 %all-reduce.8.cloned.1.call-done = bf16[1,2,32,1024]{3,2,1,0:T(8,128)(2,1)} async-done(((bf16[1,2,32,1024]{3,2,1,0:T(8,128)(2,1)}), bf16[1,2,32,1024]{3,2,1,0:T(8,128)(2,1)}) %all-reduce.8.cloned.1.call-update) | async-done | bytes 131088 | tf_op jit(solution)/shard_map/while/body/eval_jaxpr/psum | solution.py:28
  206.7 78.1 %all-reduce.8.cloned.1.call-done = bf16[1,2,32,1024]{3,2,1,0:T(8,128)(2,1)} async-done(((bf16[1,2,32,1024]{3,2,1,0:T(8,128)(2,1)}), bf16[1,2,32,1024]{3,2,1,0:T(8,128)(2,1)}) %all-reduce.8.cloned.1.call-update) | async-done | bytes 131088 | tf_op jit(solution)/shard_map/while/body/eval_jaxpr/psum | solution.py:28
  290.8 78.1 %all-reduce.8.cloned.1.call-done = bf16[1,2,32,1024]{3,2,1,0:T(8,128)(2,1)} async-done(((bf16[1,2,32,1024]{3,2,1,0:T(8,128)(2,1)}), bf16[1,2,32,1024]{3,2,1,0:T(8,128)(2,1)}) %all-reduce.8.cloned.1.call-update) | async-done | bytes 131088 | tf_op jit(solution)/shard_map/while/body/eval_jaxpr/psum | solution.py:28
  375.0 78.1 %all-reduce.8.cloned.1.call-done = bf16[1,2,32,1024]{3,2,1,0:T(8,128)(2,1)} async-done(((bf16[1,2,32,1024]{3,2,1,0:T(8,128)(2,1)}), bf16[1,2,32,1024]{3,2,1,0:T(8,128)(2,1)}) %all-reduce.8.cloned.1.call-update) | async-done | bytes 131088 | tf_op jit(solution)/shard_map/while/body/eval_jaxpr/psum | solution.py:28
  459.2 78.1 %all-reduce.8.cloned.1.call-done = bf16[1,2,32,1024]{3,2,1,0:T(8,128)(2,1)} async-done(((bf16[1,2,32,1024]{3,2,1,0:T(8,128)(2,1)}), bf16[1,2,32,1024]{3,2,1,0:T(8,128)(2,1)}) %all-reduce.8.cloned.1.call-update) | async-done | bytes 131088 | tf_op jit(solution)/shard_map/while/body/eval_jaxpr/psum | solution.py:28
  543.3 78.1 %all-reduce.8.cloned.1.call-done = bf16[1,2,32,1024]{3,2,1,0:T(8,128)(2,1)} async-done(((bf16[1,2,32,1024]{3,2,1,0:T(8,128)(2,1)}), bf16[1,2,32,1024]{3,2,1,0:T(8,128)(2,1)}) %all-reduce.8.cloned.1.call-update) | async-done | bytes 131088 | tf_op jit(solution)/shard_map/while/body/eval_jaxpr/psum | solution.py:28
  627.5 78.1 %all-reduce.8.cloned.1.call-done = bf16[1,2,32,1024]{3,2,1,0:T(8,128)(2,1)} async-done(((bf16[1,2,32,1024]{3,2,1,0:T(8,128)(2,1)}), bf16[1,2,32,1024]{3,2,1,0:T(8,128)(2,1)}) %all-reduce.8.cloned.1.call-update) | async-done | bytes 131088 | tf_op jit(solution)/shard_map/while/body/eval_jaxpr/psum | solution.py:28
  711.6 78.1 %all-reduce.8.cloned.1.call-done = bf16[1,2,32,1024]{3,2,1,0:T(8,128)(2,1)} async-done(((bf16[1,2,32,1024]{3,2,1,0:T(8,128)(2,1)}), bf16[1,2,32,1024]{3,2,1,0:T(8,128)(2,1)}) %all-reduce.8.cloned.1.call-update) | async-done | bytes 131088 | tf_op jit(solution)/shard_map/while/body/eval_jaxpr/psum | solution.py:28
  795.4 2.8 fusion.39
  802.0 9.5 collective-permute-start.2
  815.4 271.4 %all-reduce.6.cloned.1.call-done = f32[1024,3,3,128]{3,2,1,0:T(4,128)} async-done(((f32[1024,3,3,128]{3,2,1,0:T(4,128)}), f32[1024,3,3,128]{3,2,1,0:T(4,128)}) %all-reduce.6.cloned.1.call-update) | async-done | bytes 4718608
  1087.9 81.1 %all-gather.2.cloned.1.call-done = bf16[1024,3,3,128]{3,0,2,1:T(8,128)(2,1)} async-done(((bf16[32,3,3,128]{3,0,2,1:T(8,128)(2,1)}), bf16[1024,3,3,128]{3,0,2,1:T(8,128)(2,1)}) %all-gather.2.cloned.1.call-update) | async-done | bytes 2359312 | tf_op jit(solution)/shard_map/all_gather | solution.py:118
  1169.0 5.1 convolution_bitcast_fusion.2
  1179.7 2.7 fusion.108
  1183.4 24.3 %reduce-scatter.2.cloned.1.call-done = f32[128,3,3,32]{0,3,2,1:T(8,128)} async-done(((f32[1024,3,3,32]{0,3,2,1:T(8,128)}), f32[128,3,3,32]{0,3,2,1:T(8,128)}) %reduce-scatter.2.cloned.1.call-update) | async-done | bytes 147472 | tf_op jit(solution)/shard_map/reduce_scatter | solution.py:120
  1207.7 5.2 convolution_bitcast_fusion
  1212.9 156.0 %all-reduce.9 = (f32[32,3,128]{2,1,0:T(4,128)S(1)}, bf16[3,128,3,1024]{1,3,2,0:T(8,128)(2,1)}) all-reduce(f32[32,3,128]{2,1,0:T(4,128)S(1)} %constant_dynamic-update-slice_fusion.1, f32[3,128,3,1024]{1,3,2,0:T(8,128)} %convolution_bitcast_fusion), channel_id=1, replica_groups=mesh['dp'=32,'tensor'=8] {'dp'}, use_global_device_ids=true, to_apply=%region_32.33 | all-reduce | flops 1191936 | bytes 7176192 | tf_op jit(solution)/shard_map/psum | solution.py:88
  1368.9 4.3 copy.36
  (263 shorter events, 59.5 us)
Async XLA Ops:
  8.0 787.3 %copy-start = (bf16[3,128,3,1024]{3,1,2,0:T(8,128)(2,1)S(1)}, bf16[3,128,3,1024]{3,1,2,0:T(8,128)(2,1)}, u32[]{:S(2)}) copy-start(bf16[3,128,3,1024]{3,1,2,0:T(8,128)(2,1)} %param.14) | copy-start | bytes 7077892
  10.3 11.1 collective-permute-start
  14.8 6.6 collective-permute-start.1
  19.5 778.6 %copy-start.50 = (f32[128]{0:T(128)}, f32[128]{0:T(128)S(1)}, u32[]{:S(2)}) copy-start(f32[128]{0:T(128)S(1)} %get-tuple-element.197) | copy-start | bytes 1540
  19.6 780.3 %copy-start.51 = (f32[128]{0:T(128)}, f32[128]{0:T(128)S(1)}, u32[]{:S(2)}) copy-start(f32[128]{0:T(128)S(1)} %get-tuple-element.198) | copy-start | bytes 1540
  35.3 81.2 %all-reduce.8.cloned.1.call-start = ((), (), s32[]{:S(2)}) async-start(), calls=%async_computation.4 | async-start | bytes 262144 | tf_op jit(solution)/shard_map/while/body/eval_jaxpr/psum | solution.py:28
  118.1 82.6 %all-reduce.8.cloned.1.call-start = ((), (), s32[]{:S(2)}) async-start(), calls=%async_computation.4 | async-start | bytes 262144 | tf_op jit(solution)/shard_map/while/body/eval_jaxpr/psum | solution.py:28
  202.2 82.6 %all-reduce.8.cloned.1.call-start = ((), (), s32[]{:S(2)}) async-start(), calls=%async_computation.4 | async-start | bytes 262144 | tf_op jit(solution)/shard_map/while/body/eval_jaxpr/psum | solution.py:28
  286.4 82.6 %all-reduce.8.cloned.1.call-start = ((), (), s32[]{:S(2)}) async-start(), calls=%async_computation.4 | async-start | bytes 262144 | tf_op jit(solution)/shard_map/while/body/eval_jaxpr/psum | solution.py:28
  370.5 82.6 %all-reduce.8.cloned.1.call-start = ((), (), s32[]{:S(2)}) async-start(), calls=%async_computation.4 | async-start | bytes 262144 | tf_op jit(solution)/shard_map/while/body/eval_jaxpr/psum | solution.py:28
  454.7 82.6 %all-reduce.8.cloned.1.call-start = ((), (), s32[]{:S(2)}) async-start(), calls=%async_computation.4 | async-start | bytes 262144 | tf_op jit(solution)/shard_map/while/body/eval_jaxpr/psum | solution.py:28
  538.9 82.6 %all-reduce.8.cloned.1.call-start = ((), (), s32[]{:S(2)}) async-start(), calls=%async_computation.4 | async-start | bytes 262144 | tf_op jit(solution)/shard_map/while/body/eval_jaxpr/psum | solution.py:28
  623.0 82.6 %all-reduce.8.cloned.1.call-start = ((), (), s32[]{:S(2)}) async-start(), calls=%async_computation.4 | async-start | bytes 262144 | tf_op jit(solution)/shard_map/while/body/eval_jaxpr/psum | solution.py:28
  707.2 82.6 %all-reduce.8.cloned.1.call-start = ((), (), s32[]{:S(2)}) async-start(), calls=%async_computation.4 | async-start | bytes 262144 | tf_op jit(solution)/shard_map/while/body/eval_jaxpr/psum | solution.py:28
  791.3 295.5 %all-reduce.6.cloned.1.call-start = ((), (), s32[]{:S(2)}) async-start(), calls=%async_computation.3 | async-start | bytes 12582912
  791.9 377.0 %all-gather.2.cloned.1.call-start = ((), (), s32[]{:S(2)}) async-start(), calls=%async_computation.1 | async-start | bytes 2433024 | tf_op jit(solution)/shard_map/all_gather | solution.py:118
  794.0 413.7 %reduce-scatter.2.cloned.1.call-start = ((), (), s32[]{:S(2)}) async-start(), calls=%async_computation.2 | async-start | bytes 1327104 | tf_op jit(solution)/shard_map/reduce_scatter | solution.py:120
  802.0 376.7 %collective-permute-start.2 = (bf16[16,3,128]{2,0,1:T(8,128)(2,1)}, bf16[16,3,128]{2,0,1:T(8,128)(2,1)}, u32[]{:S(2)}, u32[]{:S(2)}) collective-permute-start(bf16[16,3,128]{2,0,1:T(8,128)(2,1)} %get-tuple-element.160), channel_id=1, source_target_pairs={{0,8},{8,16},{16,24},{24,32},{32,40},{40,48},{48,56},{56,64},{64,7... | collective-permute-start | bytes 36872 | tf_op jit(solution)/shard_map/ppermute | solution.py:17
  811.5 367.3 %collective-permute-start.3 = (bf16[16,3,128]{2,0,1:T(8,128)(2,1)}, bf16[16,3,128]{2,0,1:T(8,128)(2,1)}, u32[]{:S(2)}, u32[]{:S(2)}) collective-permute-start(bf16[16,3,128]{2,0,1:T(8,128)(2,1)} %get-tuple-element.161), channel_id=1, source_target_pairs={{8,0},{16,8},{24,16},{32,24},{40,32},{48,40},{56,48},{64,56},{72,6... | collective-permute-start | bytes 36872 | tf_op jit(solution)/shard_map/ppermute | solution.py:19
  1087.8 91.8 %copy-start.7 = (f32[3,128]{1,0:T(4,128)S(1)}, f32[3,128]{1,0:T(4,128)}, u32[]{:S(2)}) copy-start(f32[3,128]{1,0:T(4,128)} %copy-done.6) | copy-start | bytes 4612
  1087.8 91.8 %copy-start.9 = (f32[3,128]{1,0:T(4,128)S(1)}, f32[3,128]{1,0:T(4,128)}, u32[]{:S(2)}) copy-start(f32[3,128]{1,0:T(4,128)} %copy-done.8) | copy-start | bytes 4612
  1087.8 91.8 %copy-start.11 = (f32[3,128]{1,0:T(4,128)S(1)}, f32[3,128]{1,0:T(4,128)}, u32[]{:S(2)}) copy-start(f32[3,128]{1,0:T(4,128)} %copy-done.10) | copy-start | bytes 4612
  1087.8 91.8 %copy-start.13 = (f32[3,128]{1,0:T(4,128)S(1)}, f32[3,128]{1,0:T(4,128)}, u32[]{:S(2)}) copy-start(f32[3,128]{1,0:T(4,128)} %copy-done.12) | copy-start | bytes 4612
  1087.8 91.8 %copy-start.15 = (f32[3,128]{1,0:T(4,128)S(1)}, f32[3,128]{1,0:T(4,128)}, u32[]{:S(2)}) copy-start(f32[3,128]{1,0:T(4,128)} %copy-done.14) | copy-start | bytes 4612
  (54 other events, 860.0 us)
Sparse Core Ops, SparseCore 0:
  39.8 76.6 all-reduce.7
  122.6 77.9 all-reduce.7
  206.8 77.9 all-reduce.7
  291.0 77.9 all-reduce.7
  375.1 77.9 all-reduce.7
  459.3 77.9 all-reduce.7
  543.4 77.9 all-reduce.7
  627.6 77.9 all-reduce.7
  711.8 77.9 all-reduce.7
Sparse Core Ops, SparseCore 1:
  794.5 292.3 all-reduce.5
  1089.8 79.1 all-gather.1
  1174.1 33.5 reduce-scatter.1
where the time goes:
time: 1390 us; the launch traced here: 1380 us
  waiting for transfers between devices  1080 us (78%)
  blocking collectives  156 us (11%)
  local copies, waits for them, and re-layouts  52.2 us (4%)
  loops' own time  23.1 us (2%)
  other arithmetic  19.2 us (1%)
  starting transfers between devices  17.9 us (1%)
  between operations  17.3 us (1%)
  matrix products  16 us (1%)
    psum x9, waiting for transfers between devices, broadcast(): return lax.psum(block, axis)  702 us
    unnamed x4, waiting for transfers between devices  272 us
    psum x1, blocking collectives, per_device(): kernel_grad = lax.psum(jnp.stack(kernel_terms), 'dp') / utterances  156 us
    all_gather x1, waiting for transfers between devices, per_device(): left_full = lax.all_gather(left_piece, 'dp', axis=0, tiled=True)  81.1 us
  transfers between devices with their start and end apart: 16, of which 12 were waited for; matrix products, arithmetic and copies ran while one was open for 2% of the time, Pallas kernels for 0%

commit v1 on v0

v1 whole, which is shorter than its diff:
```python
import functools

import jax
import jax.numpy as jnp
from jax import lax
from jax.experimental import pallas as pl
from jax.experimental.pallas import tpu as pltpu
from jax.sharding import PartitionSpec as P

LEN = 2048
MESH = pl.DeviceIdType.MESH
BF = jnp.bfloat16
F32 = jnp.float32

Z = 8
QUADS = 4
TENSOR = 8
TAPS = 32
HALF = TAPS // 2
ROWS = 128
BLOCK = 1024
NB = 3
NBLK = 9
COLS = BLOCK // 2
QUART = BLOCK // 4
SHARE = LEN / (ROWS * Z * QUADS)

ORDER = (4, 3, 5, 2, 6, 1, 7, 0)
SPOT = {off: k for k, off in enumerate(ORDER)}
HOPS = ((4, 3), (3, 4))


def dot(a, b, dims):
    return lax.dot_general(a, b, (dims, ((), ())), preferred_element_type=F32)


def keep(dst, at, src, m):
    dst[at] = src[m]


def kernel(
    home, glu, weight_hbm, cot, roots, taps, gain, shift,
    upd, kgrad, igrad,
    tapf, cand, rpick, lpick, rrows, rfull, lfull, lturn,
    halo, cg_halo, gext, normed_s, at_s, cg_b, cgext, weight,
    gsend, gsib, gown, rs_send, rs_recv, e_send, e_recv,
    ysend, yrecv, gfull, wall,
    kpart, kin1, ksend2, kin2, ksum, kz, khalf,
    w_sem, halo_s, halo_r, s1_s, s1_r, r2_s, r2_r, l2_s, l2_r,
    r3_s, r3_r, l3_s, l3_r, gs_s, gs_r, rs_s, rs_r, es_s, es_r,
    y_s, y_r, c_s, c_r, wt_s, wt_r, uy_s, uy_r, uz_s, uz_r, us_s, us_r,
    ez_s, ez_r, ch_s, ch_r, k_s, k_r,
):
    d = lax.axis_index("dp")
    t = lax.axis_index("tensor")
    z = lax.div(d, 4)
    a = lax.rem(d, 4)
    yh = lax.div(a, 2)
    c = lax.rem(a, 2)
    sib = d + 1 - 2 * c
    par = d + 2 - 4 * yh

    def at_z(zz):
        return lax.rem(zz + 2 * Z, Z) * 4 + a

    z_dn, z_up = at_z(z - 1), at_z(z + 1)
    sends = []

    def send(src, dst, ss, rs, dev, when=None, start=True):
        copy = pltpu.make_async_remote_copy(
            src_ref=src, dst_ref=dst, send_sem=ss, recv_sem=rs,
            device_id=dev, device_id_type=MESH,
        )
        if when is None:
            copy.start()
        else:
            pl.when(when)(copy.start)
        sends.append((copy, when))

    def got(dst, rs):
        pltpu.make_async_remote_copy(
            src_ref=dst, dst_ref=dst, send_sem=s1_s.at[0], recv_sem=rs,
            device_id=(sib, t), device_id_type=MESH,
        ).wait_recv()

    barrier = pltpu.get_barrier_semaphore()

    def hello(dev):
        pl.semaphore_signal(barrier, inc=1, device_id=dev, device_id_type=MESH)

    hello((lax.rem(d + 31, 32), t))
    hello((lax.rem(d + 1, 32), t))
    for m in range(1, 4):
        hello((z * 4 + lax.rem(a + m, 4), t))
    for m in range(1, Z):
        hello((at_z(z + m), t))
    for m in range(1, TENSOR):
        hello((d, lax.rem(t + m, TENSOR)))

    r_to = lax.div(z, 2)
    r_slot = lax.rem(z, 2) * 4 + a

    for n in range(Z):
        pl.when(8 * a + n != d)(functools.partial(hello, (8 * a + n, t)))

    w_copy = pltpu.make_async_copy(weight_hbm, weight, w_sem)
    w_copy.start()

    left_ok = (d != 0) & (lax.rem(d * ROWS + LEN // 2, LEN) != 0)
    right_ok = (d != 31) & (lax.rem((d + 1) * ROWS + LEN // 2, LEN) != 0)
    for i in range(NB):
        gext[i, HALF:HALF + ROWS, :] = glu[i].astype(F32)
        tapf[i] = taps[i].astype(F32)

    pl.semaphore_wait(barrier, 2 + 3 + Z - 1 + TENSOR - 1 + Z - jnp.where(r_to == a, 1, 0))

    dn, up = (lax.rem(d + 31, 32), t), (lax.rem(d + 1, 32), t)
    send(glu.at[:, 0:HALF], halo.at[1], halo_s.at[0], halo_r.at[1], dn, left_ok)
    send(glu.at[:, ROWS - HALF:ROWS], halo.at[0], halo_s.at[1], halo_r.at[0], up, right_ok)
    for m in range(1, TENSOR):
        tt = lax.rem(t + m, TENSOR)
        share_cols = pl.ds(pl.multiple_of(tt * ROWS, ROWS), ROWS)
        send(roots.at[:, :, :, share_cols], cand.at[t], s1_s.at[m], s1_r.at[m], (d, tt))
    cand[t] = roots[:, :, :, pl.ds(pl.multiple_of(t * ROWS, ROWS), ROWS)]

    def rim(side, ok, sem, src, dst, rows):
        @pl.when(ok)
        def _():
            got(src.at[side], sem.at[side])
            for i in range(NB):
                dst[i, rows, :] = src[side, i].astype(F32)

        @pl.when(jnp.logical_not(ok))
        def _():
            for i in range(NB):
                dst[i, rows, :] = jnp.zeros((HALF, ROWS), F32)

    low, high = pl.ds(0, HALF), pl.ds(HALF + ROWS, HALF)
    rim(0, left_ok, halo_r, halo, gext, low)
    rim(1, right_ok, halo_r, halo, gext, high)

    def conv(i, carry):
        total = jnp.zeros((ROWS, ROWS), F32)
        for j in range(TAPS):
            total = total + tapf[i, j:j + 1, :] * gext[i, j:j + ROWS, :]
        normed = total * gain[i] + shift[i]
        normed_s[i] = normed
        at_s[i] = (normed * jax.nn.sigmoid(normed)).T.astype(BF)
        return carry

    lax.fori_loop(0, NB, conv, 0)

    own_cols = pl.ds(pl.multiple_of(c * COLS, COLS), COLS)
    sib_cols = pl.ds(pl.multiple_of((1 - c) * COLS, COLS), COLS)
    sequence = (0, 1, 2, 8, 3, 4, 5, 6, 7)
    for k in sequence:
        block = jnp.int32(8) if k == 8 else lax.rem(z + ORDER[k], Z)
        row = lax.div(block, NB)
        col = lax.rem(block, NB)
        left = at_s[row]
        gsend[k] = dot(left, cot[col, :, sib_cols], ((1,), (0,))).astype(BF)
        send(gsend.at[k], gsib.at[k], gs_s.at[k], gs_r.at[k], (sib, t))
        gown[k] = dot(left, cot[col, :, own_cols], ((1,), (0,)))

    home_z = z == 0
    for m in range(1, TENSOR):
        got(cand.at[lax.rem(t + m, TENSOR)], s1_r.at[TENSOR - m])
    r_rows = pl.ds(pl.multiple_of(r_slot * 32, 32), 32)
    for m in range(NBLK):
        x = m // Z
        zz = 0 if x else lax.rem(z + m, Z)
        slot = home[8 if x else zz]
        own, which = lax.shift_right_logical(slot, 1), slot & 1
        lpick[m] = cand[own, which, 0]
        rpick[m] = cand[own, which, 1]
        r_dev = zz * 4 + r_to
        l_dev = zz * 4 + a
        send(rpick.at[m], rrows.at[x, r_rows], r2_s.at[m], r2_r.at[x, r_slot], (r_dev, t), r_dev != d)
        pl.when(r_dev == d)(functools.partial(keep, rrows, (x, r_rows), rpick, m))
        send(lpick.at[m], lfull.at[x, z, a], l2_s.at[m], l2_r.at[x, z], (l_dev, t), l_dev != d)
        pl.when(l_dev == d)(functools.partial(keep, lfull, (x, z, a), lpick, m))

    def pair_sum(k):
        got(gsib.at[k], gs_r.at[k])
        gown[k] = gown[k] + gsib[k].astype(F32)

    def ring_step(s):
        for h, hops in enumerate(HOPS):
            for way in (0, 1):
                if s >= hops[way]:
                    continue
                off = (Z - hops[0] + s) % Z if way == 0 else hops[1] - s
                rows = slice(64 * h, 64 * h + 64)
                total = gown[SPOT[off], rows, :]
                if s > 0:
                    got(rs_recv.at[h, way, s - 1], rs_r.at[h, way, s - 1])
                    total = total + rs_recv[h, way, s - 1].astype(F32)
                rs_send[h, way, s] = total.astype(BF)
                send(
                    rs_send.at[h, way, s], rs_recv.at[h, way, s],
                    rs_s.at[h, way, s], rs_r.at[h, way, s],
                    (z_dn if way == 0 else z_up, t),
                )

    def extra_step_5():
        @pl.when(z == 5)
        def _():
            e_send[...] = gown[8].astype(BF)

        send(e_send, e_recv.at[0], es_s.at[0], es_r.at[0], (6 * 4 + a, t), z == 5)

    def extra_turn(s):
        zz = 5 + s

        @pl.when(z == zz)
        def _():
            got(e_recv.at[0], es_r.at[0])
            e_send[...] = (gown[8] + e_recv[0].astype(F32)).astype(BF)

        land = 1 if zz == 7 else 0
        send(e_send, e_recv.at[land], es_s.at[0], es_r.at[land], (((zz + 1) % Z) * 4 + a, t), z == zz)

    def extra_down(s):
        zz = 4 - s

        @pl.when(z == zz)
        def _():
            total = gown[8]
            if s > 0:
                got(e_recv.at[0], es_r.at[0])
                total = total + e_recv[0].astype(F32)
            e_send[...] = total.astype(BF)

        send(e_send, e_recv.at[0], es_s.at[0], es_r.at[0], ((zz - 1) * 4 + a, t), z == zz)

    for k in (0, 1, 2):
        pair_sum(k)
    ring_step(0)
    pair_sum(8)
    extra_down(0)
    extra_step_5()

    w_copy.wait()
    for i in range(NB):
        grad = jnp.zeros((ROWS, ROWS), F32)
        for j in range(NB):
            grad = grad + dot(cot[j], weight[i, j], ((1,), (1,)))
        normed = normed_s[i]
        sg = jax.nn.sigmoid(normed)
        cg = (grad * sg * (1.0 + normed * (1.0 - sg)) * gain[i]).astype(BF)
        cg_b[i] = cg
        cgext[i, HALF:HALF + ROWS, :] = cg.astype(F32)
    send(cg_b.at[:, 0:HALF], cg_halo.at[1], ch_s.at[0], ch_r.at[1], dn, left_ok)
    send(cg_b.at[:, ROWS - HALF:ROWS], cg_halo.at[0], ch_s.at[1], ch_r.at[0], up, right_ok)

    for k in (3, 4):
        pair_sum(k)
    ring_step(1)
    extra_down(1)
    extra_turn(1)

    def tap_grad(i, carry):
        cg = cgext[i, HALF:HALF + ROWS, :]
        for j in range(TAPS):
            terms = (cg * gext[i, j:j + ROWS, :]).reshape(ROWS // 8, 8, ROWS)
            row = jnp.sum(jnp.sum(terms, axis=0), axis=0, keepdims=True)
            kpart[j // HALF, i, j % HALF:j % HALF + 1, :] = row
        return carry

    lax.fori_loop(0, NB, tap_grad, 0)
    send(kpart.at[1 - c], kin1, k_s.at[0], k_r.at[0], (sib, t))

    for k in (5, 6):
        pair_sum(k)
    ring_step(2)
    extra_down(2)
    extra_turn(2)

    my_cols = pl.ds(pl.multiple_of(t * ROWS, ROWS), ROWS)

    def roots_in(x):
        for n in range(Z):
            source = 8 * a + n
            rows = pl.ds(32 * n, 32)
            pl.when(source != d)(functools.partial(got, rrows.at[x, rows], r2_r.at[x, n]))
            pl.when(z != n)(functools.partial(got, lfull.at[x, n, a], l2_r.at[x, n]))
        rfull[x, :, my_cols] = rrows[x]

    def roots_out(x, when):
        for m in range(1, TENSOR):
            dev = (d, lax.rem(t + m, TENSOR))
            send(rrows.at[x], rfull.at[x, :, my_cols], r3_s.at[x, m], r3_r.at[x, m], dev, when)
        for m in range(1, QUADS):
            dev = (z * 4 + lax.rem(a + m, QUADS), t)
            send(lfull.at[x, :, a], lfull.at[x, :, a], l3_s.at[x, m], l3_r.at[x, m], dev, when)

    roots_in(0)
    roots_out(0, None)
    pl.when(home_z)(functools.partial(roots_in, 1))
    roots_out(1, home_z)

    got(kin1, k_r.at[0])
    ksend2[...] = kpart[c] + kin1[...]
    send(ksend2, kin2, k_s.at[1], k_r.at[1], (par, t))

    pair_sum(7)
    ring_step(3)
    extra_down(3)

    def shares():
        for h, hops in enumerate(HOPS):
            rows = slice(64 * h, 64 * h + 64)
            total = gown[7, rows, :]
            for way in (0, 1):
                last = hops[way] - 1
                got(rs_recv.at[h, way, last], rs_r.at[h, way, last])
                total = total + rs_recv[h, way, last].astype(F32)
            gown[7, rows, :] = total
            ysend[0, rows, :] = total.astype(BF)

    shares()
    send(ysend.at[0], yrecv.at[0], y_s.at[0], y_r.at[0], (par, t))

    @pl.when(home_z)
    def _():
        total = gown[8]
        for way in (0, 1):
            got(e_recv.at[way], es_r.at[way])
            total = total + e_recv[way].astype(F32)
        gown[8] = total
        ysend[1] = total.astype(BF)

    send(ysend.at[1], yrecv.at[1], y_s.at[1], y_r.at[1], (par, t), home_z)

    got(kin2, k_r.at[1])
    ksum[...] = ksend2[...] + kin2[...]
    for m in range(1, Z):
        send(ksum, kz.at[z], k_s.at[1 + m], k_r.at[1 + m], (at_z(z + m), t))
    kz[z] = ksum[...]

    def join(x):
        got(yrecv.at[x], y_r.at[x])
        gfull[x, c] = (gown[7 + x] + yrecv[x].astype(F32)).astype(BF)

    join(0)
    send(gfull.at[0, c], gfull.at[0, c], c_s.at[0], c_r.at[0], (sib, t))

    @pl.when(home_z)
    def _():
        join(1)

    send(gfull.at[1, c], gfull.at[1, c], c_s.at[1], c_r.at[1], (sib, t), home_z)

    def roots_all(x):
        for m in range(1, TENSOR):
            tt = lax.rem(t + m, TENSOR)
            cols = pl.ds(pl.multiple_of(tt * ROWS, ROWS), ROWS)
            got(rfull.at[x, :, cols], r3_r.at[x, TENSOR - m])
        for m in range(1, QUADS):
            got(lfull.at[x, :, lax.rem(a + m, QUADS)], l3_r.at[x, QUADS - m])
        for zz in range(Z):
            part = lfull[x, zz].reshape(ROWS, ROWS).astype(F32)
            lturn[x, :, ROWS * zz:ROWS * zz + ROWS] = part.T.astype(BF)

    roots_all(0)
    got(gfull.at[0, 1 - c], c_r.at[0])

    def right(x):
        part = dot(gfull[x, 0], rfull[x, :, :COLS], ((1,), (1,)))
        part = part + dot(gfull[x, 1], rfull[x, :, COLS:], ((1,), (1,)))
        wall[x, t] = (part * SHARE).astype(BF)

    right(0)
    for m in range(1, TENSOR):
        dev = (d, lax.rem(t + m, TENSOR))
        send(wall.at[0, t], wall.at[0, t], wt_s.at[0, m], wt_r.at[0, m], dev)

    @pl.when(home_z)
    def _():
        roots_all(1)
        got(gfull.at[1, 1 - c], c_r.at[1])
        right(1)

    for m in range(1, TENSOR):
        dev = (d, lax.rem(t + m, TENSOR))
        send(wall.at[1, t], wall.at[1, t], wt_s.at[1, m], wt_r.at[1, m], dev, home_z)

    rim(0, left_ok, ch_r, cg_halo, cgext, low)
    rim(1, right_ok, ch_r, cg_halo, cgext, high)

    def back(i, carry):
        total = jnp.zeros((ROWS, ROWS), F32)
        for j in range(TAPS):
            total = total + tapf[i, j:j + 1, :] * cgext[i, TAPS - j:TAPS - j + ROWS, :]
        igrad[i] = total
        return carry

    lax.fori_loop(0, NB, back, 0)

    def quarter(block, q):
        cols = pl.ds(pl.multiple_of(q * QUART, QUART), QUART)
        return upd.at[lax.div(block, NB), lax.rem(block, NB), :, cols]

    def left_mult(x, block):
        for m in range(1, TENSOR):
            got(wall.at[x, lax.rem(t + m, TENSOR)], wt_r.at[x, TENSOR - m])
        part = dot(lturn[x], wall[x].reshape(BLOCK, QUART), ((1,), (0,)))
        quarter(block, a)[...] = part.astype(BF)

    ap = a + 2 - 4 * yh
    second = jnp.int32(Z)

    left_mult(0, z)
    send(quarter(z, a), quarter(z, a), uy_s.at[0], uy_r.at[0], (par, t))

    quarters = (c, 2 + c)

    def piece(off, h):
        return quarter(lax.rem(z + off, Z), quarters[h])

    def share(off, h):
        send(piece(off, h), piece(off, h), us_s.at[off, h], us_r.at[off, h], (sib, t))

    def spread(s):
        for h, hops in enumerate(HOPS):
            for way in (0, 1):
                if s >= hops[way]:
                    continue
                off = s if way == 0 else (Z - s) % Z
                land = off + 1 if way == 0 else (off - 1) % Z
                send(
                    piece(off, h), piece(off, h), uz_s.at[h, way, s], uz_r.at[h, land],
                    (z_dn if way == 0 else z_up, t),
                )

    @pl.when(home_z)
    def _():
        left_mult(1, second)

    send(quarter(second, a), quarter(second, a), uy_s.at[1], uy_r.at[1], (par, t), home_z)
    got(quarter(z, ap), uy_r.at[0])
    spread(0)

    def extra_spread(s):
        for h in range(2):
            src = quarter(second, quarters[h])
            send(src, src, ez_s.at[h, 0], ez_r.at[h], ((s + 1) * 4 + a, t), z == s)
            if s < 3:
                far = (Z - s) % Z
                send(src, src, ez_s.at[h, 1], ez_r.at[h], ((7 - s) * 4 + a, t), z == far)

    @pl.when(home_z)
    def _():
        got(quarter(second, ap), uy_r.at[1])

    extra_spread(0)
    for h in range(2):
        share(0, h)
        src = quarter(second, quarters[h])
        send(src, src, us_s.at[8, h], us_r.at[8, h], (sib, t), home_z)

    for s in range(1, 5):
        for h, hops in enumerate(HOPS):
            if s <= hops[0]:
                got(piece(s, h), uz_r.at[h, s])
            if s <= hops[1]:
                got(piece(Z - s, h), uz_r.at[h, Z - s])
        if s < 4:
            spread(s)
        at = (z == s) | (z == Z - s)

        @pl.when(at)
        def _():
            for h in range(2):
                got(quarter(second, quarters[h]), ez_r.at[h])

        if s < 4:
            extra_spread(s)
        for h, hops in enumerate(HOPS):
            if s <= hops[0]:
                share(s, h)
            if s <= hops[1]:
                share(Z - s, h)
            src = quarter(second, quarters[h])
            send(src, src, us_s.at[8, h], us_r.at[8, h], (sib, t), at)
        if s == 2:
            for m in range(1, Z):
                got(kz.at[lax.rem(z + m, Z)], k_r.at[1 + Z - m])
            total = kz[0]
            for zz in range(1, Z):
                total = total + kz[zz]
            khalf[c] = total * SHARE
            send(khalf.at[c], khalf.at[c], k_s.at[9], k_r.at[9], (sib, t))

    got(khalf.at[1 - c], k_r.at[9])
    for half in range(2):
        for i in range(NB):
            kgrad[i, HALF * half:HALF * half + HALF, :] = khalf[half, i]

    other = (1 - c, 3 - c)
    for h in range(2):
        for off in range(Z):
            got(quarter(lax.rem(z + off, Z), other[h]), us_r.at[off, h])
        got(quarter(second, other[h]), us_r.at[8, h])
    for copy, when in sends:
        if when is None:
            copy.wait_send()
        else:
            pl.when(when)(copy.wait_send)


def per_device(
    glu_input, conv_kernel, norm_gain, norm_shift, out_weight, out_cotangent, root_stack, home
):
    lin = glu_input[:, 0].astype(F32)
    gate_sig = jax.nn.sigmoid(glu_input[:, 1].astype(F32))
    glu_out = (lin * gate_sig).astype(BF).transpose(1, 0, 2)

    vmem = pl.BlockSpec(memory_space=pltpu.VMEM)
    dma = pltpu.SemaphoreType.DMA
    sq = (NB, ROWS, ROWS)
    out = pl.pallas_call(
        kernel,
        out_shape=(
            jax.ShapeDtypeStruct((NB, NB, ROWS, BLOCK), BF),
            jax.ShapeDtypeStruct((NB, TAPS, ROWS), F32),
            jax.ShapeDtypeStruct(sq, F32),
        ),
        in_specs=[
            pl.BlockSpec(memory_space=pltpu.SMEM), vmem, pl.BlockSpec(memory_space=pl.ANY),
            vmem, vmem, vmem, vmem, vmem,
        ],
        out_specs=(vmem, vmem, vmem),
        scratch_shapes=[
            pltpu.VMEM((NB, TAPS, ROWS), F32),
            pltpu.VMEM((TENSOR, 2, 2, 32, ROWS), BF),
            pltpu.VMEM((NBLK, 32, ROWS), BF),
            pltpu.VMEM((NBLK, 32, ROWS), BF),
            pltpu.VMEM((2, QUART, ROWS), BF),
            pltpu.VMEM((2, QUART, BLOCK), BF),
            pltpu.VMEM((2, Z, QUADS, 32, ROWS), BF),
            pltpu.VMEM((2, ROWS, BLOCK), BF),
            pltpu.VMEM((2, NB, HALF, ROWS), BF),
            pltpu.VMEM((2, NB, HALF, ROWS), BF),
            pltpu.VMEM((NB, ROWS + TAPS, ROWS), F32),
            pltpu.VMEM(sq, F32),
            pltpu.VMEM(sq, BF),
            pltpu.VMEM(sq, BF),
            pltpu.VMEM((NB, ROWS + TAPS, ROWS), F32),
            pltpu.VMEM((NB, NB, ROWS, BLOCK), BF),
            pltpu.VMEM((NBLK, ROWS, COLS), BF),
            pltpu.VMEM((NBLK, ROWS, COLS), BF),
            pltpu.VMEM((NBLK, ROWS, COLS), F32),
            pltpu.VMEM((2, 2, 4, 64, COLS), BF),
            pltpu.VMEM((2, 2, 4, 64, COLS), BF),
            pltpu.VMEM((ROWS, COLS), BF),
            pltpu.VMEM((2, ROWS, COLS), BF),
            pltpu.VMEM((2, ROWS, COLS), BF),
            pltpu.VMEM((2, ROWS, COLS), BF),
            pltpu.VMEM((2, 2, ROWS, COLS), BF),
            pltpu.VMEM((2, TENSOR, ROWS, QUART), BF),
            pltpu.VMEM((2, NB, HALF, ROWS), F32),
            pltpu.VMEM((NB, HALF, ROWS), F32),
            pltpu.VMEM((NB, HALF, ROWS), F32),
            pltpu.VMEM((NB, HALF, ROWS), F32),
            pltpu.VMEM((NB, HALF, ROWS), F32),
            pltpu.VMEM((Z, NB, HALF, ROWS), F32),
            pltpu.VMEM((2, NB, HALF, ROWS), F32),
            dma,
            dma((2,)), dma((2,)),
            dma((8,)), dma((8,)),
            dma((9,)), dma((2, 8)),
            dma((9,)), dma((2, 8)),
            dma((2, 8)), dma((2, 8)),
            dma((2, 4)), dma((2, 4)),
            dma((9,)), dma((9,)),
            dma((2, 2, 4)), dma((2, 2, 4)),
            dma((2,)), dma((2,)),
            dma((2,)), dma((2,)),
            dma((2,)), dma((2,)),
            dma((2, 8)), dma((2, 8)),
            dma((2,)), dma((2,)),
            dma((2, 2, 4)), dma((2, 8)),
            dma((9, 2)), dma((9, 2)),
            dma((2, 2)), dma((2,)),
            dma((2,)), dma((2,)),
            dma((10,)), dma((10,)),
        ],
        compiler_params=pltpu.CompilerParams(
            collective_id=0, has_side_effects=True, vmem_limit_bytes=48 * 2**20
        ),
    )(
        home, glu_out, out_weight.transpose(0, 2, 1, 3), out_cotangent.transpose(1, 0, 2),
        root_stack, conv_kernel.transpose(1, 0, 2), norm_gain[:, None], norm_shift[:, None],
    )
    update, kernel_grad, input_grad = out
    input_grad = input_grad.transpose(1, 0, 2)
    glu_grad = jnp.stack(
        [input_grad * gate_sig, input_grad * lin * gate_sig * (1.0 - gate_sig)], axis=1
    ).astype(BF)
    return glu_grad, kernel_grad.transpose(1, 0, 2), update.transpose(0, 2, 1, 3)


def solution(mesh):
    placed = (
        P("dp", None, None, "tensor"),
        P(None, None, "tensor"),
        P(None, "tensor"),
        P(None, "tensor"),
        P(None, "tensor", None, None),
        P("dp", None, None),
        P("tensor", None, "dp", None),
        P(),
    )
    return jax.shard_map(
        per_device,
        mesh=mesh,
        in_specs=placed,
        out_specs=(
            P("dp", None, None, "tensor"),
            P(None, None, "tensor"),
            P(None, "tensor", None, None),
        ),
        check_vma=False,
    )
```

time: 1390 us -> 107 us (0.08)
  waiting for transfers between devices: 1080 us -> 0 us
  blocking collectives: 156 us -> 0 us
  Pallas kernels: 0 us -> 95.4 us
  local copies, waits for them, and re-layouts: 52.2 us -> 10.8 us
  loops' own time: 23.1 us -> 0 us
  other arithmetic: 19.2 us -> 0.18 us
  starting transfers between devices: 17.9 us -> 0 us
  between operations: 17.3 us -> 0.68 us
  matrix products: 16 us -> 0 us
    psum x9 -> x0, waiting for transfers between devices: 702 us -> none  [broadcast(): return lax.psum(block, axis)]
    unnamed x4 -> x0, waiting for transfers between devices: 272 us -> none
    psum x1 -> x0, blocking collectives: 156 us -> none  [per_device(): kernel_grad = lax.psum(jnp.stack(kernel_terms), 'dp') / utterances]
    pallas_call x0 -> x1, Pallas kernels: none -> 95.4 us  [per_device(): pl.pallas_call(kernel, out_shape=(jax.ShapeDtypeStruct((NB, NB, ROWS, BLO...]
    all_gather x1 -> x0, waiting for transfers between devices: 81.1 us -> none  [per_device(): left_full = lax.all_gather(left_piece, 'dp', axis=0, tiled=True)]
    reduce_scatter x1 -> x0, waiting for transfers between devices: 24.3 us -> none  [per_device(): lax.psum_scatter(jnp.einsum('kijr,cjir->kijc', rows_now, grad_share, prec...]
    another operation x1 -> x0, loops' own time: 23.1 us -> none  [per_device(): chosen = lax.fori_loop(0, n_pairs, fetch_block, empty)]
    ppermute x4 -> x0, starting transfers between devices: 17.8 us -> none  [the longest x2 13.9 us: padded(): lax.ppermute(tail, axis, [(i, (i + 1) % count) for i in range(ends)])]
  transfers between devices with their start and end apart: 16 -> 0, of which waited for: 12 -> 0; matrix products, arithmetic and copies ran while one was open for 2% -> 0% of each run, Pallas kernels for 0% -> 0%
where the time goes in v1:
time: 107 us
  Pallas kernels  95.4 us (89%)
  local copies, waits for them, and re-layouts  10.8 us (10%)
    pallas_call x1, Pallas kernels, per_device(): pl.pallas_call(kernel, out_shape=(jax.ShapeDtypeStruct((NB, NB, ROWS, BLO...  95.4 us
    unnamed x13, local copies, waits for them, and re-layouts  8.04 us

profile of v1, /device:TPU:9, one launch (start us, length us, event | category | flops | bytes accessed | tf_op | source)
XLA Modules:
  0.0 107.1 jit_solution(772138988685394356)
XLA Ops:
  0.6 0.7 broadcast_in_dim.6.gain
  1.3 0.7 broadcast_in_dim.7.shift
  2.0 1.4 %fusion.8 = (bf16[128,1,3,128]{3,1,2,0:T(2,128)(2,1)S(1)}, bf16[128,1,3,128]{3,1,2,0:T(2,128)(2,1)S(1)}) fusion(bf16[128,2,3,128]{3,1,2,0:T(2,128)(2,1)} %param.8), kind=kLoop, calls=%fused_computation.15 | loop fusion | bytes 393216 | tf_op jit(solution)/shard_map/slice | solution.py:516
  3.4 0.1 fusion.7.glu
  3.4 0.0 copy-start
  3.4 1.7 %copy-done = bf16[3,128,3,1024]{3,1,2,0:T(8,128)(2,1)S(1)} copy-done((bf16[3,128,3,1024]{3,1,2,0:T(8,128)(2,1)S(1)}, bf16[3,128,3,1024]{3,1,2,0:T(8,128)(2,1)}, u32[]{:S(2)}) %copy-start) | copy-done | bytes 2359320
  5.1 0.0 copy-start.1
  5.1 1.1 %copy-done.1 = bf16[128,3,1024]{2,0,1:T(8,128)(2,1)S(1)} copy-done((bf16[128,3,1024]{2,0,1:T(8,128)(2,1)S(1)}, bf16[128,3,1024]{2,0,1:T(8,128)(2,1)}, u32[]{:S(2)}) %copy-start.1) | copy-done | bytes 786456
  6.2 0.0 copy-start.2
  6.2 0.9 copy-done.2
  7.2 0.0 copy-start.3
  7.2 0.7 copy-done.3
  7.9 0.0 copy-start.4
  7.9 0.7 copy-done.4
  8.6 95.4 %shard_map.103 = (bf16[3,3,128,1024]{3,2,1,0:T(8,128)(2,1)S(1)}, f32[3,32,128]{2,1,0:T(8,128)S(1)}, f32[3,128,128]{2,1,0:T(8,128)S(1)}) custom-call(s32[9]{0:T(128)S(1)} %copy-done.4, bf16[3,128,128]{2,1,0:T(8,128)(2,1)S(1)} %fusion.7.glu, bf16[3,3,128,1024]{3,2,1,0:T(8,128)(2,1)S(1)} %bitcast.41, bf16[3,128,1024]{2,1,0:T(8,128)(2,1)S(1)} %bitcast.42, ...), custom_call_target="tpu_custom_call" | custom-call | tf_op jit(solution)/shard_map/pallas_call | solution.py:522
  104.0 0.1 fusion.5
  104.2 0.9 copy.13
  105.0 0.6 copy.30
  105.7 1.4 %copy.31 = bf16[3,128,3,1024]{3,1,2,0:T(8,128)(2,1)} copy(bf16[3,128,3,1024]{3,1,2,0:T(8,128)(2,1)S(1)} %bitcast.40) | data formatting | bytes 4718592
  (1 shorter events, 0.0 us)
Async XLA Ops:
  3.4 1.7 %copy-start = (bf16[3,128,3,1024]{3,1,2,0:T(8,128)(2,1)S(1)}, bf16[3,128,3,1024]{3,1,2,0:T(8,128)(2,1)}, u32[]{:S(2)}) copy-start(bf16[3,128,3,1024]{3,1,2,0:T(8,128)(2,1)} %param.12) | copy-start | bytes 7077892
  5.1 1.1 %copy-start.1 = (bf16[128,3,1024]{2,0,1:T(8,128)(2,1)S(1)}, bf16[128,3,1024]{2,0,1:T(8,128)(2,1)}, u32[]{:S(2)}) copy-start(bf16[128,3,1024]{2,0,1:T(8,128)(2,1)} %param.13) | copy-start | bytes 2359300
  6.2 0.9 copy-start.2
  7.2 0.7 copy-start.3
  7.9 0.7 copy-start.4
